TPU v7x, 128 devices: a whole 4x4x4 slice. The times are simulated.
128 devices in a mesh: chan: 16 (over x, y_hi, core), win: 8 (over y_lo, z).
Axes of the slice: x: 4, y: 4 (y_hi: 2, y_lo: 2; y = y_hi * 2 + y_lo), z: 4, core: 2. Of those that a mesh axis runs over, the one named last changes fastest.
Arguments:
- record: bfloat16 [3, 2048, 65536], P(None, 'chan', 'win'), may hold values from -6 to 6
- chan_taps: float32 [33], replicated, may hold values from -1 to 1
- time_taps: float32 [65], replicated, may hold values from -0.75 to 0.75
- sources: int32 [3, 4], replicated, may hold values from 0 to 2047
Outputs:
- stacked: float32 [3, 4, 129, 2048], P(None, None, None, 'chan')
Inputs may be any that keep to these rules, and one draw needn't show every extreme that they name: `sources`: channel numbers of the fibre.
All inputs are finite; a program needn't handle non-finite values.
Results may differ from a plain program's by a relative error of at most 0.006.
Values may be sent and summed in bfloat16 or wider, within the bound.
A program may use at most 128 MiB of HBM per device.

v0:
```python
import math

import jax
import jax.numpy as jnp
from jax import lax
from jax.sharding import PartitionSpec as P

LAG = 64


def padded_2(cells, sides, width):
    for axis, dim in sides:
        count = lax.axis_size(axis)
        ends = count - 1
        head = lax.slice_in_dim(cells, 0, width, axis=dim)
        tail = lax.slice_in_dim(cells, cells.shape[dim] - width, cells.shape[dim], axis=dim)
        cells = jnp.concatenate(
            [
                lax.ppermute(tail, axis, [(i, (i + 1) % count) for i in range(ends)]),
                cells,
                lax.ppermute(head, axis, [((i + 1) % count, i) for i in range(ends)]),
            ],
            axis=dim,
        )
    return cells


def tap_lookup(offset, tap_table):
    count_taps = tap_table.shape[0]
    marks = offset[..., None] == lax.iota(jnp.int32, count_taps)
    picked = jnp.where(marks, tap_table.astype(jnp.float32), jnp.zeros((), jnp.float32))
    return jnp.sum(picked, axis=-1).astype(tap_table.dtype)


def band_matrix(tap_table, height, breadth):
    offset = lax.iota(jnp.int32, breadth)[None, :] - lax.iota(jnp.int32, height)[:, None]
    return tap_lookup(offset, tap_table)


def time_filter(chan_pass, tap_table):
    channels_here, samples = chan_pass.shape
    half = (tap_table.shape[0] - 1) // 2
    blocks = chan_pass.reshape(channels_here, samples // 128, 128)
    zeros_block = jnp.zeros_like(blocks[:, :1])
    earlier = jnp.concatenate([zeros_block, blocks[:, :-1]], axis=1)
    later = jnp.concatenate([blocks[:, 1:], zeros_block], axis=1)
    extended = jnp.concatenate([earlier, blocks, later], axis=2)
    offset = lax.iota(jnp.int32, 384)[:, None] - 128 - lax.iota(jnp.int32, 128)[None, :] + half
    weights = tap_lookup(offset, tap_table)
    result = jnp.einsum("cbr,rt->cbt", extended, weights, preferred_element_type=jnp.float32)
    return result.reshape(channels_here, samples)


def whiten(time_pass):
    power = jnp.mean(time_pass * time_pass, axis=-1, keepdims=True)
    return (time_pass * lax.rsqrt(power + 1e-06)).astype(jnp.bfloat16)


def correlate(whitened, panel):
    samples = whitened.shape[1]
    padded = jnp.pad(panel, ((0, 0), (LAG, LAG)))
    shifted = jnp.stack(
        [padded[:, 2 * LAG - j : 2 * LAG - j + samples] for j in range(2 * LAG + 1)], axis=1
    )
    return jnp.einsum("cu,kju->kjc", whitened, shifted, preferred_element_type=jnp.float32)


def chan_filter(piece, tap_table):
    channels_here = piece.shape[0]
    half = (tap_table.shape[0] - 1) // 2
    widened = padded_2(piece, (("chan", 0),), half)
    total = jnp.dot(
        band_matrix(tap_table, channels_here, channels_here + 2 * half),
        widened,
        preferred_element_type=jnp.float32,
    )
    return total.astype(jnp.bfloat16)


def body(record, chan_taps, time_taps, sources):
    count_steps = record.shape[0]
    channels_here = record.shape[1]
    samples = record.shape[2]
    chan_table = chan_taps.astype(jnp.bfloat16)
    time_table = time_taps.astype(jnp.bfloat16)
    first_chan = lax.axis_index("chan") * channels_here
    selector = (
        (sources - first_chan)[:, :, None] == lax.iota(jnp.int32, channels_here)[None, None, :]
    ).astype(jnp.bfloat16)
    normalizer = 1.0 / math.sqrt(samples * lax.axis_size("win"))
    pairs = []
    for section in range(count_steps):
        whitened = whiten(time_filter(chan_filter(record[section], chan_table), time_table))
        panel = lax.psum(
            jnp.dot(selector[section], whitened, preferred_element_type=jnp.float32).astype(
                jnp.bfloat16
            ),
            "chan",
        )
        pairs.append((whitened, panel))
    partial_corr = [correlate(pair[0], pair[1]) for pair in pairs]
    summed = jnp.stack([lax.psum(term, "win") for term in partial_corr])
    return summed * normalizer


def solution(mesh):
    in_specs = (P(None, "chan", "win"), P(), P(), P())
    out_specs = P(None, None, None, "chan")
    return jax.shard_map(body, mesh=mesh, in_specs=in_specs, out_specs=out_specs, check_vma=False)
```

profile of v0, /device:TPU:0, one launch (start us, length us, event | category | flops | bytes accessed | tf_op | source)
XLA Modules:
  0.0 501.7 jit_solution(6671072922488441117)
XLA Ops:
  6.5 2.3 slice_bitcast_fusion.8
  8.8 2.0 collective-permute-start
  10.8 5.9 %collective-permute-start.4 = (bf16[16,8192]{1,0:T(8,128)(2,1)S(1)}, bf16[16,8192]{1,0:T(8,128)(2,1)}, u32[]{:S(2)}, u32[]{:S(2)}) collective-permute-start(bf16[16,8192]{1,0:T(8,128)(2,1)S(1)} %get-tuple-element.12), channel_id=1, source_target_pairs={{0,8},{8,16},{16,24},{24,32},{32,40},{40,48},{48,56},{56,64},{64,7... | collective-permute-start | bytes 786440 | tf_op jit(solution)/shard_map/ppermute | solution.py:19
  16.7 1.3 collective-permute-start.3
  18.0 3.7 collective-permute-start.2
  21.8 1.3 collective-permute-start.1
  23.1 5.5 %slice_bitcast_fusion.2 = (bf16[128,8192]{1,0:T(8,128)(2,1)}, bf16[128,8192]{1,0:T(8,128)(2,1)S(1)}, bf16[128,8192]{1,0:T(8,128)(2,1)}) fusion(bf16[3,128,8192]{2,1,0:T(8,128)(2,1)} %param.4), kind=kLoop, calls=%fused_computation.86 | loop fusion | bytes 12582912 | tf_op jit(solution)/shard_map/squeeze | solution.py:93
  28.8 1.4 select_reduce_fusion
  30.6 1.7 collective-permute-start.5
  32.4 2.4 fusion.69
  35.5 1.7 fusion.75
  37.8 1.8 fusion.72
  40.2 1.5 fusion.118
  41.7 2.6 multiply_reduce_fusion.1
  44.3 1.5 fusion.119
  45.8 2.7 multiply_reduce_fusion
  49.0 1.4 convolution_convert_fusion.4
  51.0 1.3 convolution_convert_fusion.3
  52.3 1.5 fusion.117
  53.8 2.7 multiply_reduce_fusion.2
  56.5 2.0 copy-done.5
  59.1 1.3 convolution_convert_fusion.5
  60.5 5.6 %copy.25 = f32[128,8192]{1,0:T(8,128)} copy(f32[128,8192]{0,1:T(8,128)} %bitcast.872) | data formatting | bytes 8388608 | tf_op jit(solution)/shard_map/reshape | solution.py:51
  66.1 5.6 %copy.37 = f32[128,8192]{1,0:T(8,128)} copy(f32[128,8192]{0,1:T(8,128)} %bitcast.871) | data formatting | bytes 8388608 | tf_op jit(solution)/shard_map/reshape | solution.py:51
  71.7 5.6 %copy.31 = f32[128,8192]{1,0:T(8,128)} copy(f32[128,8192]{0,1:T(8,128)} %bitcast.870) | data formatting | bytes 8388608 | tf_op jit(solution)/shard_map/reshape | solution.py:51
  77.3 124.5 %all-reduce.16.cloned.1.call-done = (bf16[4,8192]{1,0:T(4,128)(2,1)}, bf16[4,8192]{1,0:T(4,128)(2,1)}, bf16[4,8192]{1,0:T(4,128)(2,1)}) async-done(((bf16[4,8192]{1,0:T(4,128)(2,1)}, bf16[4,8192]{1,0:T(4,128)(2,1)}, bf16[4,8192]{1,0:T(4,128)(2,1)}), (bf16[4,8192]{1,0:T(4,128)(2,1)}, bf16[4,8192]{1,0:T(4,128)(2,1)}, bf16[4,8192]{1,0:T(4,128)(2,1)})) %all-reduce.16.cloned.1.call-update) | async-done | bytes 196624 | tf_op jit(solution)/shard_map/psum | solution.py:94
  201.8 1.0 constant_dynamic-update-slice_fusion.386
  203.8 1.0 constant_dynamic-update-slice_fusion.384
  204.7 1.0 constant_dynamic-update-slice_fusion.383
  205.7 1.0 constant_dynamic-update-slice_fusion.382
  206.7 1.0 constant_dynamic-update-slice_fusion.381
  207.6 1.0 constant_dynamic-update-slice_fusion.380
  208.6 1.0 constant_dynamic-update-slice_fusion.379
  209.6 1.0 constant_dynamic-update-slice_fusion.378
  210.5 1.0 constant_dynamic-update-slice_fusion.377
  211.5 1.0 constant_dynamic-update-slice_fusion.376
  212.4 1.0 constant_dynamic-update-slice_fusion.375
  213.4 1.0 constant_dynamic-update-slice_fusion.374
  214.4 1.0 constant_dynamic-update-slice_fusion.373
  215.3 1.0 constant_dynamic-update-slice_fusion.372
  216.3 1.0 constant_dynamic-update-slice_fusion.371
  217.3 1.0 constant_dynamic-update-slice_fusion.370
  218.2 1.0 constant_dynamic-update-slice_fusion.369
  219.2 1.0 constant_dynamic-update-slice_fusion.368
  220.2 1.0 constant_dynamic-update-slice_fusion.367
  221.1 1.0 constant_dynamic-update-slice_fusion.366
  222.1 1.0 constant_dynamic-update-slice_fusion.365
  223.1 1.0 constant_dynamic-update-slice_fusion.364
  224.0 1.0 constant_dynamic-update-slice_fusion.363
  225.9 1.0 constant_dynamic-update-slice_fusion.361
  238.5 1.0 constant_dynamic-update-slice_fusion.348
  240.4 1.0 constant_dynamic-update-slice_fusion.346
  242.3 1.0 constant_dynamic-update-slice_fusion.344
  244.3 1.0 constant_dynamic-update-slice_fusion.342
  256.8 1.0 constant_dynamic-update-slice_fusion.329
  258.7 1.0 constant_dynamic-update-slice_fusion.327
  260.7 1.0 constant_dynamic-update-slice_fusion.325
  262.6 1.0 constant_dynamic-update-slice_fusion.323
  381.9 10.5 %fusion.88 = f32[1,4,129,128]{3,2,1,0:T(8,128)} fusion(f32[128,8192]{1,0:T(8,128)S(1)} %copy-done.8, f32[128]{0:T(128)S(1)} %add_rsqrt_fusion, bf16[4,129,8192]{2,0,1:T(4,128)(2,1)S(1)} %constant_dynamic-update-slice_fusion.258), kind=kOutput, calls=%fused_computation.92 | convolution fusion | flops 1084227584 | bytes 12913152 | tf_op jit(solution)/shard_map/cu,kju->kjc/dot_general | solution.py:65
  393.2 10.3 %fusion.83 = f32[1,4,129,128]{3,2,1,0:T(8,128)} fusion(f32[128,8192]{1,0:T(8,128)S(1)} %copy-done.7, f32[128]{0:T(128)S(1)} %add_rsqrt_fusion.1, bf16[4,129,8192]{2,0,1:T(4,128)(2,1)S(1)} %get-tuple-element.33), kind=kOutput, calls=%fused_computation.91 | convolution fusion | flops 1084227584 | bytes 12913152 | tf_op jit(solution)/shard_map/cu,kju->kjc/dot_general | solution.py:65
  403.6 13.7 %fusion.78 = f32[1,4,129,128]{3,2,1,0:T(8,128)} fusion(f32[128,8192]{1,0:T(8,128)S(1)} %copy-done.6, f32[128]{0:T(128)S(1)} %add_rsqrt_fusion.2, bf16[4,129,8192]{2,0,1:T(4,128)(2,1)} %get-tuple-element.32), kind=kOutput, calls=%fused_computation.90 | convolution fusion | flops 1084227584 | bytes 12913152 | tf_op jit(solution)/shard_map/cu,kju->kjc/dot_general | solution.py:65
  417.3 75.2 %all-reduce.14.cloned.1.call-done = (f32[1,4,129,128]{3,2,1,0:T(8,128)}, f32[1,4,129,128]{3,2,1,0:T(8,128)}, f32[1,4,129,128]{3,2,1,0:T(8,128)}) async-done(((f32[1,4,129,128]{3,2,1,0:T(8,128)}, f32[1,4,129,128]{3,2,1,0:T(8,128)}, f32[1,4,129,128]{3,2,1,0:T(8,128)}), (f32[1,4,129,128]{3,2,1,0:T(8,128)}, f32[1,4,129,128]{3,2,1,0:T(8,128)}, f32[1,4,129,128]{3,2,1,0:T(8,128)})) %all-reduce.14.cloned.1.call-update) | async-done | bytes 792592 | tf_op jit(solution)/shard_map/psum | solution.py:102
  492.4 1.2 maximum_multiply_fusion
  493.6 1.1 copy.39
  (406 shorter events, 153.6 us)
Async XLA Ops:
  6.5 22.0 %copy-start.11 = (f32[33]{0:T(128)S(1)}, f32[33]{0:T(128)}, u32[]{:S(2)}) copy-start(f32[33]{0:T(128)} %param.5) | copy-start | bytes 400
  6.5 22.0 %copy-start.12 = (f32[65]{0:T(128)S(1)}, f32[65]{0:T(128)}, u32[]{:S(2)}) copy-start(f32[65]{0:T(128)} %param.6) | copy-start | bytes 784
  6.5 22.2 %copy-start.10 = (s32[3,4]{1,0:T(4,128)S(1)}, s32[3,4]{1,0:T(4,128)}, u32[]{:S(2)}) copy-start(s32[3,4]{1,0:T(4,128)} %param.7) | copy-start | bytes 148
  6.5 195.2 %all-reduce.16.cloned.1.call-start = ((), (), s32[]{:S(2)}) async-start(), calls=%async_computation.1 | async-start | bytes 393216 | tf_op jit(solution)/shard_map/psum | solution.py:94
  8.8 21.8 %collective-permute-start = (bf16[16,8192]{1,0:T(8,128)(2,1)}, bf16[16,8192]{1,0:T(8,128)(2,1)}, u32[]{:S(2)}, u32[]{:S(2)}) collective-permute-start(bf16[16,8192]{1,0:T(8,128)(2,1)} %get-tuple-element.11), channel_id=1, source_target_pairs={{0,8},{8,16},{16,24},{24,32},{32,40},{40,48},{48,56},{56,64},{64,7... | collective-permute-start | bytes 786440 | tf_op jit(solution)/shard_map/ppermute | solution.py:19
  10.8 24.5 %collective-permute-start.4 = (bf16[16,8192]{1,0:T(8,128)(2,1)S(1)}, bf16[16,8192]{1,0:T(8,128)(2,1)}, u32[]{:S(2)}, u32[]{:S(2)}) collective-permute-start(bf16[16,8192]{1,0:T(8,128)(2,1)S(1)} %get-tuple-element.12), channel_id=1, source_target_pairs={{0,8},{8,16},{16,24},{24,32},{32,40},{40,48},{48,56},{56,64},{64,7... | collective-permute-start | bytes 786440 | tf_op jit(solution)/shard_map/ppermute | solution.py:19
  16.7 21.1 %collective-permute-start.3 = (bf16[16,8192]{1,0:T(8,128)(2,1)S(1)}, bf16[16,8192]{1,0:T(8,128)(2,1)}, u32[]{:S(2)}, u32[]{:S(2)}) collective-permute-start(bf16[16,8192]{1,0:T(8,128)(2,1)S(1)} %get-tuple-element.13), channel_id=1, source_target_pairs={{8,0},{16,8},{24,16},{32,24},{40,32},{48,40},{56,48},{64,56},{72,6... | collective-permute-start | bytes 786440 | tf_op jit(solution)/shard_map/ppermute | solution.py:21
  18.0 19.8 %collective-permute-start.2 = (bf16[16,8192]{1,0:T(8,128)(2,1)S(1)}, bf16[16,8192]{1,0:T(8,128)(2,1)}, u32[]{:S(2)}, u32[]{:S(2)}) collective-permute-start(bf16[16,8192]{1,0:T(8,128)(2,1)S(1)} %get-tuple-element.14), channel_id=1, source_target_pairs={{0,8},{8,16},{16,24},{24,32},{32,40},{40,48},{48,56},{56,64},{64,7... | collective-permute-start | bytes 786440 | tf_op jit(solution)/shard_map/ppermute | solution.py:19
  21.8 10.6 %collective-permute-start.1 = (bf16[16,8192]{1,0:T(8,128)(2,1)}, bf16[16,8192]{1,0:T(8,128)(2,1)}, u32[]{:S(2)}, u32[]{:S(2)}) collective-permute-start(bf16[16,8192]{1,0:T(8,128)(2,1)} %get-tuple-element.15), channel_id=1, source_target_pairs={{8,0},{16,8},{24,16},{32,24},{40,32},{48,40},{56,48},{64,56},{72,6... | collective-permute-start | bytes 786440 | tf_op jit(solution)/shard_map/ppermute | solution.py:21
  28.7 6.8 %copy-start.9 = (bf16[128,8192]{1,0:T(8,128)(2,1)S(1)}, bf16[128,8192]{1,0:T(8,128)(2,1)}, u32[]{:S(2)}) copy-start(bf16[128,8192]{1,0:T(8,128)(2,1)} %get-tuple-element.19) | copy-start | bytes 6291460
  30.6 4.9 collective-permute-start.5
  44.3 4.2 copy-start.3
  48.5 3.8 copy-start.4
  56.5 2.0 copy-start.5
  60.4 432.0 %all-reduce.14.cloned.1.call-start = ((), (), s32[]{:S(2)}) async-start(), calls=%async_computation | async-start | bytes 1671168 | tf_op jit(solution)/shard_map/psum | solution.py:102
  201.8 62.6 %copy-start.2 = (bf16[4,8192]{1,0:T(4,128)(2,1)S(1)}, bf16[4,8192]{1,0:T(4,128)(2,1)}, u32[]{:S(2)}) copy-start(bf16[4,8192]{1,0:T(4,128)(2,1)} %get-tuple-element.8) | copy-start | bytes 196612
  201.8 70.7 %copy-start = (bf16[4,8192]{1,0:T(4,128)(2,1)S(1)}, bf16[4,8192]{1,0:T(4,128)(2,1)}, u32[]{:S(2)}) copy-start(bf16[4,8192]{1,0:T(4,128)(2,1)} %get-tuple-element.9) | copy-start | bytes 196612
  272.3 16.5 %copy-start.1 = (bf16[4,8192]{1,0:T(4,128)(2,1)S(1)}, bf16[4,8192]{1,0:T(4,128)(2,1)}, u32[]{:S(2)}) copy-start(bf16[4,8192]{1,0:T(4,128)(2,1)} %get-tuple-element.10) | copy-start | bytes 196612
  288.7 93.2 %copy-start.8 = (f32[128,8192]{1,0:T(8,128)S(1)}, f32[128,8192]{1,0:T(8,128)}, u32[]{:S(2)}) copy-start(f32[128,8192]{1,0:T(8,128)} %copy.37) | copy-start | bytes 12582916
  376.8 16.4 %copy-start.7 = (f32[128,8192]{1,0:T(8,128)S(1)}, f32[128,8192]{1,0:T(8,128)}, u32[]{:S(2)}) copy-start(f32[128,8192]{1,0:T(8,128)} %copy.31) | copy-start | bytes 12582916
  392.4 11.1 %copy-start.6 = (f32[128,8192]{1,0:T(8,128)S(1)}, f32[128,8192]{1,0:T(8,128)}, u32[]{:S(2)}) copy-start(f32[128,8192]{1,0:T(8,128)} %copy.25) | copy-start | bytes 12582916
Sparse Core Ops, SparseCore 0:
  60.6 141.1 all-reduce.15
  417.4 74.9 all-reduce.13
where the time goes:
time: 508 us; the launch traced here: 502 us
  local copies, waits for them, and re-layouts  214 us (42%)
  waiting for transfers between devices  200 us (39%)
  matrix products  52.4 us (10%)
  starting transfers between devices  16 us (3%)
  between operations  14.6 us (3%)
    unnamed x410, local copies, waits for them, and re-layouts  181 us
    psum x1, waiting for transfers between devices, body(): lax.psum(jnp.dot(selector[section], whitened, preferred_element_type=jnp....  124 us
    psum x1, waiting for transfers between devices, body(): summed = jnp.stack([lax.psum(term, 'win') for term in partial_corr])  75.2 us
    dot_general x3, matrix products, correlate(): jnp.einsum('cu,kju->kjc', whitened, shifted, preferred_element_type=jnp.f...  34.5 us
    reshape x3, local copies, waits for them, and re-layouts, time_filter(): return result.reshape(channels_here, samples)  16.8 us
    ppermute x3, starting transfers between devices, padded_2(): lax.ppermute(tail, axis, [(i, (i + 1) % count) for i in range(ends)])  11.6 us
  transfers between devices with their start and end apart: 8, of which 3 were waited for; matrix products, arithmetic and copies ran while one was open for 6% of the time, Pallas kernels for 0%

commit v1 on v0

v1 whole, which is shorter than its diff:
```python
import functools

import jax
import jax.numpy as jnp
from jax import lax
from jax.experimental import pallas as pl
from jax.experimental.pallas import tpu as pltpu
from jax.sharding import PartitionSpec as P

MESH = pl.DeviceIdType.MESH
bf = jnp.bfloat16
f32 = jnp.float32
STEPS, SRC, ROWS, SAMP = 3, 4, 128, 8192
CT, TT = 33, 65
EXT = SAMP + 256
QUART = SAMP // 4
HALO_CHUNKS = ((0, SAMP),), ((0, SAMP),), ((0, SAMP // 2), (SAMP // 2, SAMP))


def chan_peer(c, w, d):
    return (lax.rem(c + d + 16, 16), w)


def win_peer(c, w, d):
    return (c, lax.rem(w + d, 8))


def group_of(c):
    return (c // 4) * 2 + lax.rem(c, 2)


def group_peer(c, w, i):
    x, y, k = c // 4, lax.rem(c // 2, 2), lax.rem(c, 2)
    return (lax.rem(x + i // 2, 4) * 4 + y * 2 + lax.rem(k + i % 2, 2), w)


def side_peer(c, w):
    y = lax.rem(c // 2, 2)
    return ((c // 4) * 4 + (1 - y) * 2 + lax.rem(c, 2), w)


def remote(src, dst, send, recv, dev):
    return pltpu.make_async_remote_copy(
        src_ref=src, dst_ref=dst, send_sem=send, recv_sem=recv, device_id=dev, device_id_type=MESH
    )


def tap_row(taps, count, width):
    lane = lax.broadcasted_iota(jnp.int32, (8, 128), 1)
    row = jnp.zeros((8, 128), f32)
    for j in range(count):
        row = jnp.where(lane == j, taps[j], row)
    return jnp.concatenate([row[:1]] + [jnp.zeros((1, width - 128), f32)], axis=1)


def skewed(row, height, shift):
    base = jnp.broadcast_to(row, (height, row.shape[1]))
    return pltpu.roll(base, shift, 1, stride=1, stride_axis=0)


def time_blocks(cp, weights, b0, b1, group):
    height = cp.shape[0]
    for b in range(b0, b1, group):
        n = min(group, b1 - b)
        lhs = jnp.concatenate(
            [cp[:, 256 * (b + u) : 256 * (b + u) + 512] for u in range(n)], axis=0
        )
        r = jnp.dot(lhs, weights, preferred_element_type=f32)
        yield b, [r[u * height : (u + 1) * height] for u in range(n)]


def kernel(
    rec, ctaps, ttaps, src, out,
    xs, cpi, cpe, wt, pm, rr, acc, wm, part, pland, ysrc, yland, pbf, pag, pcp, pwn,
    rsrc, rland, red, agl,
    loc_sem, hs, hr, ps, pr, ys, yr, gs, gr, rs_s, rs_r, as_s, as_r,
):
    c = lax.axis_index("chan")
    w = lax.axis_index("win")
    g_me = group_of(c)
    loads = [
        pltpu.make_async_copy(rec.at[s], xs.at[s, pl.ds(16, ROWS)], loc_sem.at[s])
        for s in range(STEPS)
    ]
    for ld in loads:
        ld.start()
    bar = pltpu.get_barrier_semaphore()
    pl.semaphore_signal(bar, inc=1, device_id=chan_peer(c, w, 1), device_id_type=MESH)
    pl.semaphore_signal(bar, inc=1, device_id=chan_peer(c, w, -1), device_id_type=MESH)
    pl.semaphore_signal(bar, inc=1, device_id=side_peer(c, w), device_id_type=MESH)
    for i in range(1, 8):
        pl.semaphore_signal(bar, inc=1, device_id=group_peer(c, w, i), device_id_type=MESH)
        pl.semaphore_signal(bar, inc=1, device_id=win_peer(c, w, i), device_id_type=MESH)
    pl.semaphore_wait(bar, 17)

    halos = []
    n = 0
    for s in range(STEPS):
        for lo, hi in HALO_CHUNKS[s]:
            cols = pl.ds(lo, hi - lo)
            up = remote(
                rec.at[s, pl.ds(0, 16), cols], xs.at[s, pl.ds(144, 16), cols],
                hs.at[n], hr.at[n], chan_peer(c, w, -1),
            )
            down = remote(
                rec.at[s, pl.ds(112, 16), cols], xs.at[s, pl.ds(0, 16), cols],
                hs.at[n + 1], hr.at[n + 1], chan_peer(c, w, 1),
            )
            halos.append((up, down))
            n += 2
    for pair in halos:
        for cp in pair:
            cp.start()

    zpad = jnp.zeros((96, 128), bf)
    cpi[:, 0:128] = zpad
    cpi[:, SAMP + 128 : SAMP + 256] = zpad
    zpad = jnp.zeros((32, 128), bf)
    cpe[:, 0:128] = zpad
    cpe[:, SAMP + 128 : SAMP + 256] = zpad
    for s in range(STEPS):
        wt[s, ROWS : 2 * ROWS, SAMP : SAMP + 128] = jnp.zeros((ROWS, 128), bf)
        pwn[s, :, 0:128] = jnp.zeros((8, 128), f32)
        pwn[s, 4:8, 128 : SAMP + 128] = jnp.zeros((4, SAMP), f32)
        pwn[s, :, SAMP + 128 : SAMP + 256] = jnp.zeros((8, 128), f32)

    crow = tap_row(ctaps, CT, 256)
    b_in = skewed(crow, 96, 0)[:, :128].astype(bf)
    lane16 = lax.broadcasted_iota(jnp.int32, (16, 128), 1)
    top = skewed(crow, 16, 0)[:, :128]
    low = skewed(crow, 16, 48)[:, :128]
    top = jnp.where((lane16 < 16) & (c == 0), 0.0, top)
    low = jnp.where((lane16 >= 80) & (c == 15), 0.0, low)
    b_ed = jnp.concatenate([top, low], axis=0)[:, :96].astype(bf)
    wm[...] = jnp.transpose(skewed(tap_row(ttaps, TT, 512), 256, 96)).astype(bf)

    row16 = lax.broadcasted_iota(jnp.int32, (16, 128), 0)
    quarter = lax.broadcasted_iota(jnp.int32, (16, 256), 0) // 4
    for s in range(STEPS):
        want = jnp.zeros((16, 128), jnp.int32)
        for k in range(SRC):
            want = jnp.where(lax.rem(row16, 4) == k, src[s, k], want)
        off = lane16 - (want - c * ROWS) + 16
        pick = jnp.zeros((16, 128), f32)
        for j in range(CT):
            pick = jnp.where(off == j, ctaps[j], pick)
        pick = pick.astype(bf)
        loads[s].wait()
        got = jnp.dot(pick, xs[s, 16:144, :], preferred_element_type=f32)
        for g in range(8):
            val = got[:, 256 * g : 256 * g + 256]
            for q in range(1, 4):
                o = q * QUART + 256 * g
                val = jnp.where(quarter == q, got[:, o : o + 256], val)
            part[s, g] = val
        for i in range(1, 8):
            dev = group_peer(c, w, i)
            remote(
                part.at[s, group_of(dev[0])], pland.at[s, i],
                ps.at[8 * s + i], pr.at[8 * s + i], dev,
            ).start()

    def p_copy(s, i):
        dev = group_peer(c, w, i)
        return remote(
            part.at[s, group_of(dev[0])], pland.at[s, i], ps.at[8 * s + i], pr.at[8 * s + i], dev
        )

    def y_copy(s):
        return remote(ysrc.at[s], yland.at[s], ys.at[s], yr.at[s], side_peer(c, w))

    def g_copy(s, i):
        return remote(
            pbf.at[s], pag.at[s, g_me], gs.at[8 * s + i], gr.at[8 * s + i], group_peer(c, w, i)
        )

    def whiten_into(s, row, b, results, prev):
        cols = 256 * b
        y = jnp.concatenate(results, axis=1).astype(bf)
        width = y.shape[1]
        shifted = jnp.concatenate([prev, y[:, : width - 64]], axis=1)
        at = 0
        for r0, h in row:
            wt[s, ROWS + r0 : ROWS + r0 + h, cols : cols + width] = y[at : at + h]
            wt[s, r0 : r0 + h, cols : cols + width] = shifted[at : at + h]
            at += h
        return y[:, width - 64 :]

    def finish_w(s, row, prev):
        tail = jnp.concatenate([prev, jnp.zeros((prev.shape[0], 64), bf)], axis=1)
        at = 0
        for r0, h in row:
            wt[s, r0 : r0 + h, SAMP : SAMP + 128] = tail[at : at + h]
            at += h

    inner, edges = ((16, 96),), ((0, 16), (112, 16))

    def inner_pass(s):
        cpi[:, 128 : SAMP + 128] = jnp.dot(
            b_in, xs[s, 16:144, :], preferred_element_type=f32
        ).astype(bf)
        prev = jnp.zeros((96, 64), bf)
        total = jnp.zeros((96, 256), f32)
        for b, results in time_blocks(cpi, wm[...], 0, 32, 8):
            for r in results:
                total = total + r * r
            prev = whiten_into(s, inner, b, results, prev)
        finish_w(s, inner, prev)
        acc[s, 16:112, :] = total

    def edge_chan(s, lo, hi):
        both = jnp.concatenate([xs[s, 0:48, lo:hi], xs[s, 112:160, lo:hi]], axis=0)
        cpe[:, 128 + lo : 128 + hi] = jnp.dot(b_ed, both, preferred_element_type=f32).astype(bf)

    def edge_time(s, b0, b1, state):
        prev, total = state
        for b, results in time_blocks(cpe, wm[...], b0, b1, 16):
            for r in results:
                total = total + r * r
            prev = whiten_into(s, edges, b, results, prev)
        if b1 == 32:
            finish_w(s, edges, prev)
            acc[s, 0:16, :] = total[0:16]
            acc[s, 112:128, :] = total[16:32]
        return prev, total

    def edge_state():
        return jnp.zeros((32, 64), bf), jnp.zeros((32, 256), f32)

    def panel(s):
        x0 = pag[s, 0].astype(f32)[:, 0:128]
        x7 = pag[s, 7].astype(f32)[:, 128:256]
        z4 = jnp.zeros((4, 128), f32)
        pcp[:, 0:128] = jnp.concatenate([z4, x7[0:12]], axis=0).astype(bf)
        pcp[:, QUART + 128 : QUART + 256] = jnp.concatenate([x0[4:16], z4], axis=0).astype(bf)
        for g in range(8):
            pcp[:, 128 + 256 * g : 384 + 256 * g] = pag[s, g]
        (_, res), = time_blocks(pcp, wm[...], 0, 8, 8)
        tot = res[0] * res[0]
        for r in res[1:]:
            tot = tot + r * r
        tot = jnp.sum(tot, axis=1, keepdims=True)
        tot = tot[0:4] + tot[4:8] + tot[8:12] + tot[12:16]
        scale = lax.rsqrt(tot * (1.0 / SAMP) + 1e-6)
        scale = jnp.concatenate([scale] * 4, axis=0)
        full = jnp.concatenate([(r * scale).astype(bf).astype(f32) for r in res], axis=1)
        for q in range(4):
            pwn[s, 0:4, 128 + QUART * q : 128 + QUART * (q + 1)] = full[4 * q : 4 * q + 4]

    def build_p(s):
        for lo in range(0, SAMP + 128, 2048):
            n = min(2048, SAMP + 128 - lo)
            for k in range(SRC):
                row = pwn[s, k : k + 1, lo : lo + n + 128]
                pm[64 * k : 64 * k + 64, lo : lo + n] = skewed(row, 64, 0)[:, 128:].astype(bf)
            late = pwn[s, :, lo + 64 : lo + 64 + n]
            pm[256:272, lo : lo + n] = jnp.concatenate([late, late], axis=0).astype(bf)

    def corr(s, lo, hi, first):
        d = lax.dot_general(
            pm[:, lo:hi], wt[s, :, lo:hi], (((1,), (1,)), ((), ())), preferred_element_type=f32
        )
        rr[...] = d if first else rr[...] + d

    def r_copy(s, i):
        dev = win_peer(c, w, i)
        return remote(
            rsrc.at[s, dev[1]], rland.at[s, w], rs_s.at[8 * s + i], rs_r.at[8 * s + i], dev
        )

    def a_copy(s, i):
        return remote(
            red.at[s], agl.at[s, w], as_s.at[8 * s + i], as_r.at[8 * s + i], win_peer(c, w, i)
        )

    def send_corr(s):
        power = jnp.sum(jnp.transpose(acc[s]), axis=0, keepdims=True)
        scale = lax.rsqrt(power * (1.0 / SAMP) + 1e-6)
        scale = jnp.concatenate([scale, scale], axis=1)
        val = (rr[...] * scale).astype(bf)
        for k in range(8):
            rsrc[s, k, 0:32] = val[32 * k : 32 * k + 32]
            rsrc[s, k, 32:48] = val[256:272]
        for i in range(1, 8):
            r_copy(s, i).start()
        rland[s, w] = rsrc[s, w]

    norm = 1.0 / 256.0

    def reduce_corr(s):
        for i in range(1, 8):
            r_copy(s, i).wait()
        tot = rland[s, 0].astype(f32)
        for i in range(1, 8):
            tot = tot + rland[s, i].astype(f32)
        tot = tot * norm
        mine = tot[0:32].astype(bf)
        red[s] = mine
        for i in range(1, 8):
            a_copy(s, i).start()
        agl[s, w] = mine
        for k in range(SRC):
            out[s, k, 128:129, :] = tot[32 + k : 33 + k, 128:256]

    def write_out(s):
        for i in range(1, 8):
            a_copy(s, i).wait()
        for k in range(SRC):
            for h in range(2):
                val = agl[s, 2 * k + h].astype(f32)
                out[s, k, 32 * h : 32 * h + 32, :] = val[:, 0:128]
                out[s, k, 64 + 32 * h : 96 + 32 * h, :] = val[:, 128:256]

    def reduce_panel(s):
        for i in range(1, 8):
            p_copy(s, i).wait()
        tot = part[s, g_me]
        for i in range(1, 8):
            tot = tot + pland[s, i]
        ysrc[s] = tot
        y_copy(s).start()

    def share_panel(s):
        y_copy(s).wait()
        val = (ysrc[s] + yland[s]).astype(bf)
        pbf[s] = val
        for i in range(1, 8):
            g_copy(s, i).start()
        pag[s, g_me] = val

    def wait_panel(s):
        for i in range(1, 8):
            g_copy(s, i).wait()

    def wait_halo(j):
        for cp in halos[j]:
            cp.wait()

    inner_pass(0)
    for s in range(STEPS):
        reduce_panel(s)
    inner_pass(1)
    inner_pass(2)
    for s in range(STEPS):
        share_panel(s)
    wait_halo(0)
    edge_chan(0, 0, SAMP)
    edge_time(0, 0, 32, edge_state())
    wait_panel(0)
    panel(0)
    build_p(0)
    corr(0, 0, SAMP + 128, True)
    send_corr(0)
    wait_panel(1)
    panel(1)
    build_p(1)
    wait_halo(1)
    edge_chan(1, 0, SAMP)
    edge_time(1, 0, 32, edge_state())
    corr(1, 0, SAMP + 128, True)
    send_corr(1)
    reduce_corr(0)
    wait_panel(2)
    panel(2)
    build_p(2)
    wait_halo(2)
    edge_chan(2, 0, SAMP // 2)
    state = edge_time(2, 0, 15, edge_state())
    corr(2, 0, 3840, True)
    reduce_corr(1)
    wait_halo(3)
    edge_chan(2, SAMP // 2, SAMP)
    edge_time(2, 15, 32, state)
    corr(2, 3840, SAMP + 128, False)
    send_corr(2)
    write_out(0)
    write_out(1)
    reduce_corr(2)
    write_out(2)


def body(record, chan_taps, time_taps, sources):
    vm, dma = pltpu.VMEM, pltpu.SemaphoreType.DMA
    smem = pl.BlockSpec(memory_space=pltpu.SMEM)
    return pl.pallas_call(
        kernel,
        out_shape=jax.ShapeDtypeStruct((STEPS, SRC, 129, ROWS), f32),
        in_specs=[pl.BlockSpec(memory_space=pl.ANY), smem, smem, smem],
        out_specs=pl.BlockSpec(memory_space=pltpu.VMEM),
        scratch_shapes=[
            vm((STEPS, 160, SAMP), bf),
            vm((96, EXT), bf),
            vm((32, EXT), bf),
            vm((STEPS, 256, EXT), bf),
            vm((272, EXT), bf),
            vm((272, 256), f32),
            vm((STEPS, ROWS, 256), f32),
            vm((512, 256), bf),
            vm((STEPS, 8, 16, 256), f32),
            vm((STEPS, 8, 16, 256), f32),
            vm((STEPS, 16, 256), f32),
            vm((STEPS, 16, 256), f32),
            vm((STEPS, 16, 256), bf),
            vm((STEPS, 8, 16, 256), bf),
            vm((16, QUART + 256), bf),
            vm((STEPS, 8, EXT), f32),
            vm((STEPS, 8, 48, 256), bf),
            vm((STEPS, 8, 48, 256), bf),
            vm((STEPS, 32, 256), bf),
            vm((STEPS, 8, 32, 256), bf),
            dma((STEPS,)),
            dma((8,)), dma((8,)),
            dma((24,)), dma((24,)),
            dma((STEPS,)), dma((STEPS,)),
            dma((24,)), dma((24,)),
            dma((24,)), dma((24,)),
            dma((24,)), dma((24,)),
        ],
        compiler_params=pltpu.CompilerParams(
            collective_id=0, has_side_effects=True, vmem_limit_bytes=58 * 2**20
        ),
        name="xcorr",
    )(record, chan_taps, time_taps, sources)


def solution(mesh):
    in_specs = (P(None, "chan", "win"), P(), P(), P())
    out_specs = P(None, None, None, "chan")
    return jax.shard_map(body, mesh=mesh, in_specs=in_specs, out_specs=out_specs, check_vma=False)
```

time: 508 us -> 61.8 us (0.12); the launches traced: 502 us -> 61.7 us
  local copies, waits for them, and re-layouts: 214 us -> 2.24 us
  waiting for transfers between devices: 200 us -> 0 us
  Pallas kernels: 0 us -> 59.4 us
  matrix products: 52.4 us -> 0 us
  starting transfers between devices: 16 us -> 0 us
  between operations: 14.6 us -> 0.01 us
    psum x2 -> x0, waiting for transfers between devices: 200 us -> none  [the longest x1 124 us: body(): lax.psum(jnp.dot(selector[section], whitened, preferred_element_type=jnp....]
    unnamed x410 -> x0, local copies, waits for them, and re-layouts: 181 us -> none
    pallas_call x0 -> x1, Pallas kernels: none -> 59.4 us  [body(): pl.pallas_call(kernel, out_shape=jax.ShapeDtypeStruct((STEPS, SRC, 129, R...]
    dot_general x12 -> x0, matrix products: 52.4 us -> none  [the longest x3 34.5 us: correlate(): jnp.einsum('cu,kju->kjc', whitened, shifted, preferred_element_type=jnp.f...]
    reshape x6 -> x0, local copies, waits for them, and re-layouts: 18.6 us -> none  [the longest x3 16.8 us: time_filter(): return result.reshape(channels_here, samples)]
    ppermute x6 -> x0, starting transfers between devices: 16 us -> none  [the longest x3 11.6 us: padded_2(): lax.ppermute(tail, axis, [(i, (i + 1) % count) for i in range(ends)])]
    slice x4 -> x0, local copies, waits for them, and re-layouts: 6.73 us -> none  [the longest x3 4.44 us: time_filter(): earlier = jnp.concatenate([zeros_block, blocks[:, :-1]], axis=1)]
    squeeze x1 -> x0, local copies, waits for them, and re-layouts: 5.5 us -> none  [body(): record[section]]
  transfers between devices with their start and end apart: 8 -> 0, of which waited for: 3 -> 0; matrix products, arithmetic and copies ran while one was open for 6% -> 0% of each run, Pallas kernels for 0% -> 0%
where the time goes in v1:
time: 61.8 us; the launch traced here: 61.7 us
  Pallas kernels  59.4 us (96%)
  local copies, waits for them, and re-layouts  2.24 us (4%)
    pallas_call x1, Pallas kernels, body(): pl.pallas_call(kernel, out_shape=jax.ShapeDtypeStruct((STEPS, SRC, 129, R...  59.4 us
    pallas_call x1, local copies, waits for them, and re-layouts, body(): pl.pallas_call(kernel, out_shape=jax.ShapeDtypeStruct((STEPS, SRC, 129, R...  2.24 us

profile of v1, /device:TPU:0, one launch (start us, length us, event | category | flops | bytes accessed | tf_op | source)
XLA Modules:
  0.0 61.7 jit_solution(13163793724233207887)
XLA Ops:
  0.0 59.4 %xcorr.1 = f32[3,4,129,128]{3,2,1,0:T(8,128)} custom-call(bf16[3,128,8192]{2,1,0:T(8,128)(2,1)} %rec.1, f32[33]{0:T(128)} %ctaps.1, f32[65]{0:T(128)} %ttaps.1, s32[3,4]{1,0:T(4,128)} %src.1), custom_call_target="tpu_custom_call" | custom-call | tf_op jit(solution)/shard_map/xcorr/pallas_call | solution.py:385
  59.4 2.2 %copy.5 = f32[3,4,129,128]{3,1,2,0:T(4,128)} copy(f32[3,4,129,128]{3,2,1,0:T(8,128)} %xcorr.1) | data formatting | bytes 1585152 | tf_op jit(solution)/shard_map/xcorr/pallas_call | solution.py:385

commit v2 on v1

--- a/solution.py
+++ b/solution.py
@@ -14,7 +14,10 @@
 CT, TT = 33, 65
 EXT = SAMP + 256
 QUART = SAMP // 4
-HALO_CHUNKS = ((0, SAMP),), ((0, SAMP),), ((0, SAMP // 2), (SAMP // 2, SAMP))
+HALVES = ((0, SAMP // 2), (SAMP // 2, SAMP))
+HALO_CHUNKS = (HALVES, HALVES, HALVES)
+EARLY = 2
+ORDER = (2, 0, 1)
 
 
 def chan_peer(c, w, d):
@@ -72,8 +75,8 @@
 def kernel(
     rec, ctaps, ttaps, src, out,
     xs, cpi, cpe, wt, pm, rr, acc, wm, part, pland, ysrc, yland, pbf, pag, pcp, pwn,
-    rsrc, rland, red, agl,
-    loc_sem, hs, hr, ps, pr, ys, yr, gs, gr, rs_s, rs_r, as_s, as_r,
+    zsrc, zland, vsrc, vland, red, agl, lates, wte, pm2, re, eacc, esrc, eland,
+    loc_sem, hs, hr, ps, pr, ys, yr, gs, gr, zs, zr, vs, vr, as_, ar, es, er,
 ):
     c = lax.axis_index("chan")
     w = lax.axis_index("win")
@@ -82,8 +85,8 @@
         pltpu.make_async_copy(rec.at[s], xs.at[s, pl.ds(16, ROWS)], loc_sem.at[s])
         for s in range(STEPS)
     ]
-    for ld in loads:
-        ld.start()
+    for s in ORDER:
+        loads[s].start()
     bar = pltpu.get_barrier_semaphore()
     pl.semaphore_signal(bar, inc=1, device_id=chan_peer(c, w, 1), device_id_type=MESH)
     pl.semaphore_signal(bar, inc=1, device_id=chan_peer(c, w, -1), device_id_type=MESH)
@@ -108,35 +111,14 @@
             )
             halos.append((up, down))
             n += 2
-    for pair in halos:
+    for pair in halos[:EARLY]:
         for cp in pair:
             cp.start()
 
-    zpad = jnp.zeros((96, 128), bf)
-    cpi[:, 0:128] = zpad
-    cpi[:, SAMP + 128 : SAMP + 256] = zpad
-    zpad = jnp.zeros((32, 128), bf)
-    cpe[:, 0:128] = zpad
-    cpe[:, SAMP + 128 : SAMP + 256] = zpad
-    for s in range(STEPS):
-        wt[s, ROWS : 2 * ROWS, SAMP : SAMP + 128] = jnp.zeros((ROWS, 128), bf)
-        pwn[s, :, 0:128] = jnp.zeros((8, 128), f32)
-        pwn[s, 4:8, 128 : SAMP + 128] = jnp.zeros((4, SAMP), f32)
-        pwn[s, :, SAMP + 128 : SAMP + 256] = jnp.zeros((8, 128), f32)
-
-    crow = tap_row(ctaps, CT, 256)
-    b_in = skewed(crow, 96, 0)[:, :128].astype(bf)
-    lane16 = lax.broadcasted_iota(jnp.int32, (16, 128), 1)
-    top = skewed(crow, 16, 0)[:, :128]
-    low = skewed(crow, 16, 48)[:, :128]
-    top = jnp.where((lane16 < 16) & (c == 0), 0.0, top)
-    low = jnp.where((lane16 >= 80) & (c == 15), 0.0, low)
-    b_ed = jnp.concatenate([top, low], axis=0)[:, :96].astype(bf)
-    wm[...] = jnp.transpose(skewed(tap_row(ttaps, TT, 512), 256, 96)).astype(bf)
-
     row16 = lax.broadcasted_iota(jnp.int32, (16, 128), 0)
     quarter = lax.broadcasted_iota(jnp.int32, (16, 256), 0) // 4
-    for s in range(STEPS):
+    lane16 = lax.broadcasted_iota(jnp.int32, (16, 128), 1)
+    for s in ORDER:
         want = jnp.zeros((16, 128), jnp.int32)
         for k in range(SRC):
             want = jnp.where(lax.rem(row16, 4) == k, src[s, k], want)
@@ -160,6 +142,33 @@
                 ps.at[8 * s + i], pr.at[8 * s + i], dev,
             ).start()
 
+    zpad = jnp.zeros((96, 128), bf)
+    cpi[:, 0:128] = zpad
+    cpi[:, SAMP + 128 : SAMP + 256] = zpad
+    zpad = jnp.zeros((32, 128), bf)
+    cpe[:, 0:128] = zpad
+    cpe[:, SAMP + 128 : SAMP + 256] = zpad
+    for s in range(STEPS):
+        wt[s, ROWS : 2 * ROWS, SAMP : SAMP + 128] = jnp.zeros((ROWS, 128), bf)
+        pwn[s, :, 0:128] = jnp.zeros((8, 128), f32)
+        pwn[s, 4:8, 128 : SAMP + 128] = jnp.zeros((4, SAMP), f32)
+        pwn[s, :, SAMP + 128 : SAMP + 256] = jnp.zeros((8, 128), f32)
+
+    for r0 in (0, 112, ROWS, ROWS + 112):
+        wt[2, r0 : r0 + 16, 0 : SAMP + 128] = jnp.zeros((16, SAMP + 128), bf)
+    wte[32:64, SAMP : SAMP + 128] = jnp.zeros((32, 128), bf)
+    acc[2, 0:16, :] = jnp.zeros((16, 256), f32)
+    acc[2, 112:128, :] = jnp.zeros((16, 256), f32)
+
+    crow = tap_row(ctaps, CT, 256)
+    b_in = skewed(crow, 96, 0)[:, :128].astype(bf)
+    top = skewed(crow, 16, 0)[:, :128]
+    low = skewed(crow, 16, 48)[:, :128]
+    top = jnp.where((lane16 < 16) & (c == 0), 0.0, top)
+    low = jnp.where((lane16 >= 80) & (c == 15), 0.0, low)
+    b_ed = jnp.concatenate([top, low], axis=0)[:, :96].astype(bf)
+    wm[...] = jnp.transpose(skewed(tap_row(ttaps, TT, 512), 256, 96)).astype(bf)
+
     def p_copy(s, i):
         dev = group_peer(c, w, i)
         return remote(
@@ -174,26 +183,26 @@
             pbf.at[s], pag.at[s, g_me], gs.at[8 * s + i], gr.at[8 * s + i], group_peer(c, w, i)
         )
 
-    def whiten_into(s, row, b, results, prev):
+    def store_w(dst, half, rows, b, results, prev):
         cols = 256 * b
         y = jnp.concatenate(results, axis=1).astype(bf)
         width = y.shape[1]
         shifted = jnp.concatenate([prev, y[:, : width - 64]], axis=1)
         at = 0
-        for r0, h in row:
-            wt[s, ROWS + r0 : ROWS + r0 + h, cols : cols + width] = y[at : at + h]
-            wt[s, r0 : r0 + h, cols : cols + width] = shifted[at : at + h]
+        for r0, h in rows:
+            dst[half + r0 : half + r0 + h, cols : cols + width] = y[at : at + h]
+            dst[r0 : r0 + h, cols : cols + width] = shifted[at : at + h]
             at += h
         return y[:, width - 64 :]
 
-    def finish_w(s, row, prev):
+    def finish_w(dst, rows, prev):
         tail = jnp.concatenate([prev, jnp.zeros((prev.shape[0], 64), bf)], axis=1)
         at = 0
-        for r0, h in row:
-            wt[s, r0 : r0 + h, SAMP : SAMP + 128] = tail[at : at + h]
+        for r0, h in rows:
+            dst[r0 : r0 + h, SAMP : SAMP + 128] = tail[at : at + h]
             at += h
 
-    inner, edges = ((16, 96),), ((0, 16), (112, 16))
+    inner, edges, alone = ((16, 96),), ((0, 16), (112, 16)), ((0, 32),)
 
     def inner_pass(s):
         cpi[:, 128 : SAMP + 128] = jnp.dot(
@@ -204,8 +213,8 @@
         for b, results in time_blocks(cpi, wm[...], 0, 32, 8):
             for r in results:
                 total = total + r * r
-            prev = whiten_into(s, inner, b, results, prev)
-        finish_w(s, inner, prev)
+            prev = store_w(wt.at[s], ROWS, inner, b, results, prev)
+        finish_w(wt.at[s], inner, prev)
         acc[s, 16:112, :] = total
 
     def edge_chan(s, lo, hi):
@@ -214,14 +223,18 @@
 
     def edge_time(s, b0, b1, state):
         prev, total = state
+        dst, half, rows = (wte, 32, alone) if s == 2 else (wt.at[s], ROWS, edges)
         for b, results in time_blocks(cpe, wm[...], b0, b1, 16):
             for r in results:
                 total = total + r * r
-            prev = whiten_into(s, edges, b, results, prev)
+            prev = store_w(dst, half, rows, b, results, prev)
         if b1 == 32:
-            finish_w(s, edges, prev)
-            acc[s, 0:16, :] = total[0:16]
-            acc[s, 112:128, :] = total[16:32]
+            finish_w(dst, rows, prev)
+            if s == 2:
+                eacc[...] = total
+            else:
+                acc[s, 0:16, :] = total[0:16]
+                acc[s, 112:128, :] = total[16:32]
         return prev, total
 
     def edge_state():
@@ -247,69 +260,127 @@
         for q in range(4):
             pwn[s, 0:4, 128 + QUART * q : 128 + QUART * (q + 1)] = full[4 * q : 4 * q + 4]
 
+    def build_piece(s, lo, hi):
+        dst = pm2 if s == 2 else pm
+        for k in range(SRC):
+            row = pwn[s, k : k + 1, lo : hi + 128]
+            dst[64 * k : 64 * k + 64, lo:hi] = skewed(row, 64, 0)[:, 128:].astype(bf)
+        late = pwn[s, :, lo + 64 : hi + 64]
+        dst[256:272, lo:hi] = jnp.concatenate([late, late], axis=0).astype(bf)
+
     def build_p(s):
         for lo in range(0, SAMP + 128, 2048):
-            n = min(2048, SAMP + 128 - lo)
-            for k in range(SRC):
-                row = pwn[s, k : k + 1, lo : lo + n + 128]
-                pm[64 * k : 64 * k + 64, lo : lo + n] = skewed(row, 64, 0)[:, 128:].astype(bf)
-            late = pwn[s, :, lo + 64 : lo + 64 + n]
-            pm[256:272, lo : lo + n] = jnp.concatenate([late, late], axis=0).astype(bf)
-
-    def corr(s, lo, hi, first):
-        d = lax.dot_general(
-            pm[:, lo:hi], wt[s, :, lo:hi], (((1,), (1,)), ((), ())), preferred_element_type=f32
+            build_piece(s, lo, min(lo + 2048, SAMP + 128))
+
+    def matmul_nt(lhs, rhs):
+        return lax.dot_general(lhs, rhs, (((1,), (1,)), ((), ())), preferred_element_type=f32)
+
+    def corr(s):
+        hi = SAMP + 128
+        rr[...] = matmul_nt((pm2 if s == 2 else pm)[:, 0:hi], wt[s, :, 0:hi])
+
+    def edge_corr(lo, hi, first):
+        d = matmul_nt(pm2[:, lo:hi], wte[:, lo:hi])
+        re[...] = d if first else re[...] + d
+
+    def scales(sums):
+        power = jnp.sum(jnp.transpose(sums), axis=0, keepdims=True)
+        scale = lax.rsqrt(power * (1.0 / SAMP) + 1e-6)
+        return jnp.concatenate([scale, scale], axis=1)
+
+    def z_peer(i):
+        return (c, (w // 4) * 4 + lax.rem(w + i, 4))
+
+    z_me = lax.rem(w, 4)
+
+    def z_copy(s, i):
+        dev = z_peer(i)
+        return remote(
+            zsrc.at[s, lax.rem(w + i, 4)], zland.at[s, i], zs.at[4 * s + i], zr.at[4 * s + i], dev
         )
-        rr[...] = d if first else rr[...] + d
-
-    def r_copy(s, i):
-        dev = win_peer(c, w, i)
-        return remote(
-            rsrc.at[s, dev[1]], rland.at[s, w], rs_s.at[8 * s + i], rs_r.at[8 * s + i], dev
-        )
+
+    def v_copy(s):
+        return remote(vsrc.at[s], vland.at[s], vs.at[s], vr.at[s], (c, lax.rem(w + 4, 8)))
 
     def a_copy(s, i):
-        return remote(
-            red.at[s], agl.at[s, w], as_s.at[8 * s + i], as_r.at[8 * s + i], win_peer(c, w, i)
-        )
+        return remote(red.at[s], agl.at[s, z_me], as_.at[4 * s + i], ar.at[4 * s + i], z_peer(i))
+
+    def e_copy(i):
+        return remote(esrc, eland.at[w], es.at[i], er.at[i], win_peer(c, w, i))
+
+    norm = 1.0 / 256.0
 
     def send_corr(s):
-        power = jnp.sum(jnp.transpose(acc[s]), axis=0, keepdims=True)
-        scale = lax.rsqrt(power * (1.0 / SAMP) + 1e-6)
-        scale = jnp.concatenate([scale, scale], axis=1)
-        val = (rr[...] * scale).astype(bf)
-        for k in range(8):
-            rsrc[s, k, 0:32] = val[32 * k : 32 * k + 32]
-            rsrc[s, k, 32:48] = val[256:272]
-        for i in range(1, 8):
-            r_copy(s, i).start()
-        rland[s, w] = rsrc[s, w]
-
-    norm = 1.0 / 256.0
-
-    def reduce_corr(s):
-        for i in range(1, 8):
-            r_copy(s, i).wait()
-        tot = rland[s, 0].astype(f32)
-        for i in range(1, 8):
-            tot = tot + rland[s, i].astype(f32)
+        val = rr[...] * scales(acc[s])
+        lates[s] = val[256:264, 128:256]
+        val = val.astype(bf)
+        for k in range(SRC):
+            zsrc[s, k, 0:64] = val[64 * k : 64 * k + 64]
+        for i in range(1, 4):
+            z_copy(s, i).start()
+
+    def sum_z(s):
+        for i in range(1, 4):
+            z_copy(s, i).wait()
+        tot = zsrc[s, z_me].astype(f32)
+        for i in range(1, 4):
+            tot = tot + zland[s, i].astype(f32)
+        vsrc[s] = tot.astype(bf)
+        v_copy(s).start()
+
+    def sum_y(s):
+        v_copy(s).wait()
+        val = ((vsrc[s].astype(f32) + vland[s].astype(f32)) * norm).astype(bf)
+        red[s] = val
+        for i in range(1, 4):
+            a_copy(s, i).start()
+        agl[s, z_me] = val
+
+    def wait_all(s):
+        for i in range(1, 4):
+            a_copy(s, i).wait()
+
+    def write_out(s):
+        wait_all(s)
+        for k in range(SRC):
+            out[s, k, 0:64, :] = agl[s, k, :, 0:128]
+            out[s, k, 64:128, :] = agl[s, k, :, 128:256]
+
+    def send_edges():
+        val = re[...] * scales(eacc[...])
+        fold = jnp.concatenate([val[0:128], val[128:256]], axis=1)
+        late = jnp.concatenate([val[256:260], val[256:260]], axis=1)
+        late = jnp.concatenate([late] + [lates[s][0:4] for s in range(STEPS)], axis=0)
+        val = jnp.concatenate([fold, late], axis=0).astype(bf)
+        esrc[...] = val
+        for i in range(1, 8):
+            e_copy(i).start()
+        eland[w] = val
+
+    def add_edges():
+        for i in range(1, 8):
+            e_copy(i).wait()
+        tot = eland[0].astype(f32)
+        for i in range(1, 8):
+            tot = tot + eland[i].astype(f32)
         tot = tot * norm
-        mine = tot[0:32].astype(bf)
-        red[s] = mine
-        for i in range(1, 8):
-            a_copy(s, i).start()
-        agl[s, w] = mine
+
+        def spread(rows, at):
+            mid = jnp.zeros((rows.shape[0], 96), f32)
+            return jnp.concatenate([rows[:, at : at + 16], mid, rows[:, at + 16 : at + 32]], axis=1)
+
+        blank = jnp.zeros((15, ROWS), f32)
         for k in range(SRC):
-            out[s, k, 128:129, :] = tot[32 + k : 33 + k, 128:256]
-
-    def write_out(s):
-        for i in range(1, 8):
-            a_copy(s, i).wait()
-        for k in range(SRC):
-            for h in range(2):
-                val = agl[s, 2 * k + h].astype(f32)
-                out[s, k, 32 * h : 32 * h + 32, :] = val[:, 0:128]
-                out[s, k, 64 + 32 * h : 96 + 32 * h, :] = val[:, 128:256]
+            rows = tot[64 * (k % 2) : 64 * (k % 2) + 64]
+            at = 64 * (k // 2)
+            for a in range(2):
+                val = agl[2, k, :, 128 * a : 128 * a + 128].astype(f32) + spread(rows, at + 32 * a)
+                out[2, k, 64 * a : 64 * a + 64, :] = val.astype(bf)
+            for s in range(STEPS):
+                val = tot[132 + 4 * s + k : 133 + 4 * s + k]
+                if s == 2:
+                    val = val + spread(tot[128 + k : 129 + k], 32)
+                out[s, k, 128:144, :] = jnp.concatenate([val, blank], axis=0).astype(bf)
 
     def reduce_panel(s):
         for i in range(1, 8):
@@ -336,55 +407,66 @@
         for cp in halos[j]:
             cp.wait()
 
+    inner_pass(2)
+    for s in ORDER:
+        reduce_panel(s)
+    for pair in halos[EARLY:]:
+        for cp in pair:
+            cp.start()
     inner_pass(0)
-    for s in range(STEPS):
-        reduce_panel(s)
     inner_pass(1)
-    inner_pass(2)
-    for s in range(STEPS):
+    for s in ORDER:
         share_panel(s)
     wait_halo(0)
+    wait_halo(1)
     edge_chan(0, 0, SAMP)
     edge_time(0, 0, 32, edge_state())
+    wait_panel(2)
+    panel(2)
+    build_p(2)
+    corr(2)
+    send_corr(2)
     wait_panel(0)
     panel(0)
     build_p(0)
-    corr(0, 0, SAMP + 128, True)
+    corr(0)
     send_corr(0)
     wait_panel(1)
     panel(1)
     build_p(1)
-    wait_halo(1)
+    sum_z(2)
+    wait_halo(2)
+    wait_halo(3)
     edge_chan(1, 0, SAMP)
     edge_time(1, 0, 32, edge_state())
-    corr(1, 0, SAMP + 128, True)
+    corr(1)
     send_corr(1)
-    reduce_corr(0)
-    wait_panel(2)
-    panel(2)
-    build_p(2)
-    wait_halo(2)
+    sum_z(0)
+    wait_halo(4)
     edge_chan(2, 0, SAMP // 2)
     state = edge_time(2, 0, 15, edge_state())
-    corr(2, 0, 3840, True)
-    reduce_corr(1)
-    wait_halo(3)
+    edge_corr(0, 3840, True)
+    sum_z(1)
+    sum_y(2)
+    wait_halo(5)
     edge_chan(2, SAMP // 2, SAMP)
     edge_time(2, 15, 32, state)
-    corr(2, 3840, SAMP + 128, False)
-    send_corr(2)
+    edge_corr(3840, SAMP + 128, False)
+    send_edges()
+    sum_y(0)
+    sum_y(1)
     write_out(0)
     write_out(1)
-    reduce_corr(2)
-    write_out(2)
+    wait_all(2)
+    add_edges()
 
 
 def body(record, chan_taps, time_taps, sources):
     vm, dma = pltpu.VMEM, pltpu.SemaphoreType.DMA
     smem = pl.BlockSpec(memory_space=pltpu.SMEM)
-    return pl.pallas_call(
+    packed = pl.pallas_call(
         kernel,
-        out_shape=jax.ShapeDtypeStruct((STEPS, SRC, 129, ROWS), f32),
+        out_shape=jax.ShapeDtypeStruct((STEPS, SRC, 144, ROWS), bf),
         in_specs=[pl.BlockSpec(memory_space=pl.ANY), smem, smem, smem],
         out_specs=pl.BlockSpec(memory_space=pltpu.VMEM),
         scratch_shapes=[
@@ -404,23 +486,35 @@
             vm((STEPS, 8, 16, 256), bf),
             vm((16, QUART + 256), bf),
             vm((STEPS, 8, EXT), f32),
-            vm((STEPS, 8, 48, 256), bf),
-            vm((STEPS, 8, 48, 256), bf),
-            vm((STEPS, 32, 256), bf),
-            vm((STEPS, 8, 32, 256), bf),
+            vm((STEPS, 4, 64, 256), bf),
+            vm((STEPS, 4, 64, 256), bf),
+            vm((STEPS, 64, 256), bf),
+            vm((STEPS, 64, 256), bf),
+            vm((STEPS, 64, 256), bf),
+            vm((STEPS, 4, 64, 256), bf),
+            vm((STEPS, 8, 128), f32),
+            vm((64, EXT), bf),
+            vm((272, EXT), bf),
+            vm((272, 64), f32),
+            vm((32, 256), f32),
+            vm((144, 128), bf),
+            vm((8, 144, 128), bf),
             dma((STEPS,)),
-            dma((8,)), dma((8,)),
+            dma((12,)), dma((12,)),
             dma((24,)), dma((24,)),
             dma((STEPS,)), dma((STEPS,)),
             dma((24,)), dma((24,)),
-            dma((24,)), dma((24,)),
-            dma((24,)), dma((24,)),
+            dma((12,)), dma((12,)),
+            dma((STEPS,)), dma((STEPS,)),
+            dma((12,)), dma((12,)),
+            dma((8,)), dma((8,)),
         ],
         compiler_params=pltpu.CompilerParams(
             collective_id=0, has_side_effects=True, vmem_limit_bytes=58 * 2**20
         ),
         name="xcorr",
     )(record, chan_taps, time_taps, sources)
+    return packed[:, :, :129].astype(f32)
 
 
 def solution(mesh):

time: 61.8 us -> 56.8 us (0.919)
  Pallas kernels: 59.4 us -> 54.2 us
  local copies, waits for them, and re-layouts: 2.24 us -> 1.09 us
  other arithmetic: 0 us -> 1.06 us
    pallas_call x1, Pallas kernels: 59.4 us -> 54.2 us  [body(): pl.pallas_call(kernel, out_shape=jax.ShapeDtypeStruct((STEPS, SRC, 144, R...]
    pallas_call x1 -> x0, local copies, waits for them, and re-layouts: 2.24 us -> none  [body(): pl.pallas_call(kernel, out_shape=jax.ShapeDtypeStruct((STEPS, SRC, 129, R...]
    convert_element_type x0 -> x1, local copies, waits for them, and re-layouts: none -> 1.09 us  [body(): return packed[:, :, :129].astype(f32)]
    convert_element_type x0 -> x1, other arithmetic: none -> 1.06 us  [body(): return packed[:, :, :129].astype(f32)]
where the time goes in v2:
time: 56.8 us; the launch traced here: 56.4 us
  Pallas kernels  54.2 us (95%)
  local copies, waits for them, and re-layouts  1.09 us (2%)
  other arithmetic  1.06 us (2%)
    pallas_call x1, Pallas kernels, body(): pl.pallas_call(kernel, out_shape=jax.ShapeDtypeStruct((STEPS, SRC, 144, R...  54.2 us

profile of v2, /device:TPU:0, one launch (start us, length us, event | category | flops | bytes accessed | tf_op | source)
XLA Modules:
  0.0 56.4 jit_solution(11574180627208884411)
XLA Ops:
  0.0 54.2 %xcorr.1 = bf16[3,4,144,128]{3,2,1,0:T(8,128)(2,1)} custom-call(bf16[3,128,8192]{2,1,0:T(8,128)(2,1)} %rec.1, f32[33]{0:T(128)} %ctaps.1, f32[65]{0:T(128)} %ttaps.1, s32[3,4]{1,0:T(4,128)} %src.1), custom_call_target="tpu_custom_call" | custom-call | tf_op jit(solution)/shard_map/xcorr/pallas_call | solution.py:467
  54.2 1.1 %slice_convert_fusion = f32[3,4,129,128]{3,2,1,0:T(8,128)S(1)} fusion(bf16[3,4,144,128]{3,2,1,0:T(8,128)(2,1)} %xcorr.1), kind=kLoop, calls=%fused_computation | loop fusion | flops 198144 | bytes 1188864 | tf_op jit(solution)/shard_map/convert_element_type | solution.py:517
  55.3 1.1 %copy.5 = f32[3,4,129,128]{3,1,2,0:T(4,128)} copy(f32[3,4,129,128]{3,2,1,0:T(8,128)S(1)} %slice_convert_fusion) | data formatting | bytes 1585152 | tf_op jit(solution)/shard_map/convert_element_type | solution.py:517

commit v3 on v2

--- a/solution.py
+++ b/solution.py
@@ -73,7 +73,8 @@
 
 
 def kernel(
-    rec, ctaps, ttaps, src, out,
+    rec, ctaps_in, ttaps_in, src_in, out,
+    ctaps, ttaps, src, small_sem,
     xs, cpi, cpe, wt, pm, rr, acc, wm, part, pland, ysrc, yland, pbf, pag, pcp, pwn,
     zsrc, zland, vsrc, vland, red, agl, lates, wte, pm2, re, eacc, esrc, eland,
     loc_sem, hs, hr, ps, pr, ys, yr, gs, gr, zs, zr, vs, vr, as_, ar, es, er,
@@ -87,6 +88,12 @@
     ]
     for s in ORDER:
         loads[s].start()
+    small = [
+        pltpu.make_async_copy(a, b, small_sem.at[n])
+        for n, (a, b) in enumerate(((ctaps_in, ctaps), (ttaps_in, ttaps), (src_in, src)))
+    ]
+    for cp in small:
+        cp.start()
     bar = pltpu.get_barrier_semaphore()
     pl.semaphore_signal(bar, inc=1, device_id=chan_peer(c, w, 1), device_id_type=MESH)
     pl.semaphore_signal(bar, inc=1, device_id=chan_peer(c, w, -1), device_id_type=MESH)
@@ -115,6 +122,8 @@
         for cp in pair:
             cp.start()
 
+    for cp in small:
+        cp.wait()
     row16 = lax.broadcasted_iota(jnp.int32, (16, 128), 0)
     quarter = lax.broadcasted_iota(jnp.int32, (16, 256), 0) // 4
     lane16 = lax.broadcasted_iota(jnp.int32, (16, 128), 1)
@@ -463,13 +472,17 @@
 
 def body(record, chan_taps, time_taps, sources):
     vm, dma = pltpu.VMEM, pltpu.SemaphoreType.DMA
-    smem = pl.BlockSpec(memory_space=pltpu.SMEM)
+    sm = pltpu.SMEM
     packed = pl.pallas_call(
         kernel,
         out_shape=jax.ShapeDtypeStruct((STEPS, SRC, 144, ROWS), bf),
-        in_specs=[pl.BlockSpec(memory_space=pl.ANY), smem, smem, smem],
+        in_specs=[pl.BlockSpec(memory_space=pl.ANY)] * 4,
         out_specs=pl.BlockSpec(memory_space=pltpu.VMEM),
         scratch_shapes=[
+            sm((CT,), f32),
+            sm((TT,), f32),
+            sm((STEPS, SRC), jnp.int32),
+            dma((3,)),
             vm((STEPS, 160, SAMP), bf),
             vm((96, EXT), bf),
             vm((32, EXT), bf),

time: 56.8 us -> 56.1 us (0.988)
  Pallas kernels: 54.2 us -> 53.6 us
    pallas_call x1, Pallas kernels: 54.2 us -> 53.6 us  [body(): pl.pallas_call(kernel, out_shape=jax.ShapeDtypeStruct((STEPS, SRC, 144, R...]
where the time goes in v3:
time: 56.1 us; the launch traced here: 55.7 us
  Pallas kernels  53.6 us (96%)
  local copies, waits for them, and re-layouts  1.09 us (2%)
  other arithmetic  1.06 us (2%)
    pallas_call x1, Pallas kernels, body(): pl.pallas_call(kernel, out_shape=jax.ShapeDtypeStruct((STEPS, SRC, 144, R...  53.6 us

profile of v3, /device:TPU:0, one launch (start us, length us, event | category | flops | bytes accessed | tf_op | source)
XLA Modules:
  0.0 55.7 jit_solution(6766646572228083847)
XLA Ops:
  0.0 53.6 %xcorr.1 = bf16[3,4,144,128]{3,2,1,0:T(8,128)(2,1)} custom-call(bf16[3,128,8192]{2,1,0:T(8,128)(2,1)} %rec.1, f32[33]{0:T(128)} %ctaps_in.1, f32[65]{0:T(128)} %ttaps_in.1, s32[3,4]{1,0:T(4,128)} %src_in.1), custom_call_target="tpu_custom_call" | custom-call | tf_op jit(solution)/shard_map/xcorr/pallas_call | solution.py:476
  53.6 1.1 %slice_convert_fusion = f32[3,4,129,128]{3,2,1,0:T(8,128)S(1)} fusion(bf16[3,4,144,128]{3,2,1,0:T(8,128)(2,1)} %xcorr.1), kind=kLoop, calls=%fused_computation | loop fusion | flops 198144 | bytes 1188864 | tf_op jit(solution)/shard_map/convert_element_type | solution.py:530
  54.6 1.1 %copy.5 = f32[3,4,129,128]{3,1,2,0:T(4,128)} copy(f32[3,4,129,128]{3,2,1,0:T(8,128)S(1)} %slice_convert_fusion) | data formatting | bytes 1585152 | tf_op jit(solution)/shard_map/convert_element_type | solution.py:530

commit v4 on v3

--- a/solution.py
+++ b/solution.py
@@ -16,7 +16,7 @@
 QUART = SAMP // 4
 HALVES = ((0, SAMP // 2), (SAMP // 2, SAMP))
 HALO_CHUNKS = (HALVES, HALVES, HALVES)
-EARLY = 2
+EARLY = 3
 ORDER = (2, 0, 1)
 
 

time: 56.1 us -> 56.2 us (level)
  no operation moved by 1% of the time
where the time goes in v4:
time: 56.2 us; the launch traced here: 55.8 us
  Pallas kernels  53.6 us (95%)
  local copies, waits for them, and re-layouts  1.09 us (2%)
  other arithmetic  1.06 us (2%)
    pallas_call x1, Pallas kernels, body(): pl.pallas_call(kernel, out_shape=jax.ShapeDtypeStruct((STEPS, SRC, 144, R...  53.6 us

profile of v4, /device:TPU:0, one launch (start us, length us, event | category | flops | bytes accessed | tf_op | source)
XLA Modules:
  0.0 55.8 jit_solution(14964100222150054124)
XLA Ops:
  0.0 53.6 %xcorr.1 = bf16[3,4,144,128]{3,2,1,0:T(8,128)(2,1)} custom-call(bf16[3,128,8192]{2,1,0:T(8,128)(2,1)} %rec.1, f32[33]{0:T(128)} %ctaps_in.1, f32[65]{0:T(128)} %ttaps_in.1, s32[3,4]{1,0:T(4,128)} %src_in.1), custom_call_target="tpu_custom_call" | custom-call | tf_op jit(solution)/shard_map/xcorr/pallas_call | solution.py:476
  53.6 1.1 %slice_convert_fusion = f32[3,4,129,128]{3,2,1,0:T(8,128)S(1)} fusion(bf16[3,4,144,128]{3,2,1,0:T(8,128)(2,1)} %xcorr.1), kind=kLoop, calls=%fused_computation | loop fusion | flops 198144 | bytes 1188864 | tf_op jit(solution)/shard_map/convert_element_type | solution.py:530
  54.7 1.1 %copy.5 = f32[3,4,129,128]{3,1,2,0:T(4,128)} copy(f32[3,4,129,128]{3,2,1,0:T(8,128)S(1)} %slice_convert_fusion) | data formatting | bytes 1585152 | tf_op jit(solution)/shard_map/convert_element_type | solution.py:530
